TPU v7x, 256 devices: a whole 4x4x8 slice. The times are simulated.
256 devices in a mesh: row: 16 (over y, x), col: 16 (over z, core).
Axes of the slice: x: 4, y: 4, z: 8, core: 2. Of those that a mesh axis runs over, the one named last changes fastest.
Arguments:
- tokens: bfloat16 [1024, 8192], P('col', 'row'), may hold values from -6 to 6
- out_grad: bfloat16 [1024, 8192], P('col', 'row'), may hold values from -6 to 6
- w_gate: bfloat16 [8192, 28672], P('row', 'col'), may hold values from -0.0625 to 0.0625
- w_up: bfloat16 [8192, 28672], P('row', 'col'), may hold values from -0.0625 to 0.0625
- w_down: bfloat16 [28672, 8192], P('col', 'row'), may hold values from -0.0625 to 0.0625
Outputs:
- in_grad: bfloat16 [1024, 8192], P('col', 'row')
- gate_grad: bfloat16 [8192, 28672], P('row', 'col')
- up_grad: bfloat16 [8192, 28672], P('row', 'col')
- down_grad: bfloat16 [28672, 8192], P('col', 'row')
All inputs are finite; a program needn't handle non-finite values.
Results may differ from a plain program's by a relative error of at most 0.035.
Values may be sent and summed in bfloat16 or wider, within the bound.
A program may use at most 128 MiB of HBM per device.

v0:
```python
import jax
import jax.numpy as jnp
from jax import lax
from jax.sharding import PartitionSpec as P


def contract_rows(left, right):
    return lax.dot_general(
        left, right, (((0,), (0,)), ((), ())), preferred_element_type=jnp.float32
    )


def contract_cols(left, right):
    return lax.dot_general(
        left, right, (((1,), (1,)), ((), ())), preferred_element_type=jnp.float32
    )


def make_hidden(gate, upval):
    g_val = gate.astype(jnp.float32)
    return (g_val * jax.nn.sigmoid(g_val) * upval.astype(jnp.float32)).astype(jnp.bfloat16)


def swiglu_back(gate, upval, dhid):
    g_val = gate.astype(jnp.float32)
    u_val = upval.astype(jnp.float32)
    d_val = dhid.astype(jnp.float32)
    sig = jax.nn.sigmoid(g_val)
    dgate = (d_val * u_val * sig * (1.0 + g_val * (1.0 - sig))).astype(jnp.bfloat16)
    dup = (d_val * g_val * sig).astype(jnp.bfloat16)
    return (dgate, dup)


def body(tokens, out_grad, w_gate, w_up, w_down):
    tok_full, grad_full = (
        lax.all_gather(tokens, "col", axis=0, tiled=True),
        lax.all_gather(out_grad, "col", axis=0, tiled=True),
    )
    gate_part = jnp.dot(tok_full, w_gate, preferred_element_type=jnp.float32)
    up_part = jnp.dot(tok_full, w_up, preferred_element_type=jnp.float32)
    down_part = contract_cols(grad_full, w_down)
    dhid = lax.psum_scatter(down_part.astype(jnp.bfloat16), "row", scatter_dimension=0, tiled=True)
    share_rows = dhid.shape[0]
    gate_sum, up_sum = (
        lax.psum(gate_part.astype(jnp.bfloat16), "row").astype(jnp.float32),
        lax.psum(up_part.astype(jnp.bfloat16), "row").astype(jnp.float32),
    )
    gate_all = gate_sum.astype(jnp.bfloat16)
    up_all = up_sum.astype(jnp.bfloat16)
    hidden_full = make_hidden(gate_all, up_all)
    start = lax.axis_index("row") * share_rows
    gate_rows = lax.dynamic_slice_in_dim(gate_all, start, share_rows, 0)
    up_rows = lax.dynamic_slice_in_dim(up_all, start, share_rows, 0)
    dgate, dup = swiglu_back(gate_rows, up_rows, dhid)
    dgate_full, dup_full = (
        lax.all_gather(dgate, "row", axis=0, tiled=True),
        lax.all_gather(dup, "row", axis=0, tiled=True),
    )
    down_grad = contract_rows(hidden_full, grad_full).astype(jnp.bfloat16)
    gate_grad = contract_rows(tok_full, dgate_full).astype(jnp.bfloat16)
    up_grad = contract_rows(tok_full, dup_full).astype(jnp.bfloat16)
    in_part = contract_cols(dgate_full, w_gate) + contract_cols(dup_full, w_up)
    in_grad = lax.psum_scatter(in_part.astype(jnp.bfloat16), "col", scatter_dimension=0, tiled=True)
    return (in_grad, gate_grad, up_grad, down_grad)


def solution(mesh):
    placed = (P("col", "row"), P("col", "row"), P("row", "col"), P("row", "col"), P("col", "row"))
    return jax.shard_map(
        body,
        mesh=mesh,
        in_specs=placed,
        out_specs=(P("col", "row"), P("row", "col"), P("row", "col"), P("col", "row")),
        check_vma=False,
    )
```

profile of v0, /device:TPU:1, one launch (start us, length us, event | category | flops | bytes accessed | tf_op | source)
XLA Modules:
  0.0 501.6 jit_solution(15901347693128225751)
XLA Ops:
  7.2 0.0 copy-start
  7.2 0.0 all-gather.5.cloned.1.call-start
  7.2 0.7 all-gather.5.cloned.1.call-update
  7.9 0.0 all-gather.7.cloned.1.call-start
  8.0 0.7 all-gather.7.cloned.1.call-update
  8.7 0.0 reduce-scatter.3.cloned.1.call-start
  8.7 44.0 %all-gather.5.cloned.1.call-done = bf16[1024,512]{1,0:T(8,128)(2,1)} async-done(((bf16[64,512]{1,0:T(8,128)(2,1)}), bf16[1024,512]{1,0:T(8,128)(2,1)}) %all-gather.5.cloned.1.call-update) | async-done | bytes 1048592 | tf_op jit(solution)/shard_map/all_gather | solution.py:37
  52.7 5.8 %convolution_convert_fusion.2 = bf16[1024,1792]{1,0:T(8,128)(2,1)} fusion(bf16[1024,512]{1,0:T(8,128)(2,1)} %all-gather.5.cloned.1.call-done, bf16[1792,512]{1,0:T(8,128)(2,1)} %param.9), kind=kOutput, calls=%fused_computation.9 | convolution fusion | flops 1880883200 | bytes 6553600 | tf_op jit(solution)/shard_map/dot_general | solution.py:14
  58.5 0.0 reduce-scatter.3.cloned.1.call-update
  58.5 0.0 all-reduce.3.cloned.1.call-start
  58.6 33.2 %all-gather.7.cloned.1.call-done = bf16[1024,512]{1,0:T(8,128)(2,1)} async-done(((bf16[64,512]{1,0:T(8,128)(2,1)}), bf16[1024,512]{1,0:T(8,128)(2,1)}) %all-gather.7.cloned.1.call-update) | async-done | bytes 1048592 | tf_op jit(solution)/shard_map/all_gather | solution.py:36
  91.8 0.0 copy-done
  91.8 0.0 copy-start.2
  91.8 0.0 copy-start.4
  91.8 5.2 %convolution_convert_fusion = bf16[1024,1792]{1,0:T(8,128)(2,1)} fusion(bf16[1024,512]{1,0:T(8,128)(2,1)} %all-gather.7.cloned.1.call-done, bf16[512,1792]{1,0:T(8,128)(2,1)S(1)} %copy-done), kind=kOutput, calls=%fused_computation.7 | convolution fusion | flops 1880883200 | bytes 6553600 | tf_op jit(solution)/shard_map/dot_general | solution.py:39
  97.0 0.0 copy-done.2
  97.0 0.0 copy-done.4
  97.0 4.0 convolution_convert_fusion.1
  101.0 0.0 all-reduce.3.cloned.1.call-update
  101.0 0.0 all-gather.9.cloned.1.call-start
  101.1 72.6 %reduce-scatter.3.cloned.1.call-done = bf16[64,1792]{1,0:T(8,128)(2,1)} async-done(((bf16[1024,1792]{1,0:T(8,128)(2,1)}), bf16[64,1792]{1,0:T(8,128)(2,1)}) %reduce-scatter.3.cloned.1.call-update) | async-done | bytes 229392 | tf_op jit(solution)/shard_map/reduce_scatter | solution.py:42
  173.7 146.1 %all-reduce.3.cloned.1.call-done = (bf16[1024,1792]{1,0:T(8,128)(2,1)}, bf16[1024,1792]{1,0:T(8,128)(2,1)}) async-done(((bf16[1024,1792]{1,0:T(8,128)(2,1)}, bf16[1024,1792]{1,0:T(8,128)(2,1)}), (bf16[1024,1792]{1,0:T(8,128)(2,1)}, bf16[1024,1792]{1,0:T(8,128)(2,1)})) %all-reduce.3.cloned.1.call-update) | async-done | bytes 7340048 | tf_op jit(solution)/shard_map/psum | solution.py:46
  319.8 2.2 fusion.20
  321.9 0.0 all-gather.9.cloned.1.call-update
  321.9 0.0 all-gather.11.cloned.1.call-start
  322.0 0.5 all-gather.11.cloned.1.call-update
  322.5 0.2 reduce-scatter.5.cloned.1.call-start
  322.8 54.3 %all-gather.9.cloned.1.call-done = bf16[1024,1792]{1,0:T(8,128)(2,1)} async-done(((bf16[64,1792]{1,0:T(8,128)(2,1)}), bf16[1024,1792]{1,0:T(8,128)(2,1)}) %all-gather.9.cloned.1.call-update) | async-done | bytes 3670032 | tf_op jit(solution)/shard_map/all_gather | solution.py:56
  377.1 5.4 %fusion.22 = f32[1024,512]{1,0:T(8,128)} fusion(bf16[1024,1792]{1,0:T(8,128)(2,1)} %all-gather.9.cloned.1.call-done, bf16[512,1792]{1,0:T(8,128)(2,1)S(1)} %copy-done), kind=kOutput, calls=%fused_computation.31 | convolution fusion | flops 1879048192 | bytes 7602176 | tf_op jit(solution)/shard_map/dot_general | solution.py:14
  382.5 0.0 copy-start.3
  382.5 51.7 %all-gather.11.cloned.1.call-done = bf16[1024,1792]{1,0:T(8,128)(2,1)} async-done(((bf16[64,1792]{1,0:T(8,128)(2,1)}), bf16[1024,1792]{1,0:T(8,128)(2,1)}) %all-gather.11.cloned.1.call-update) | async-done | bytes 3670032 | tf_op jit(solution)/shard_map/all_gather | solution.py:57
  434.2 6.3 %add_convert_fusion = bf16[1024,512]{1,0:T(8,128)(2,1)} fusion(f32[1024,512]{1,0:T(8,128)} %fusion.22, bf16[1024,1792]{1,0:T(8,128)(2,1)} %all-gather.11.cloned.1.call-done, bf16[512,1792]{1,0:T(8,128)(2,1)} %param.8), kind=kOutput, calls=%fused_computation.16 | convolution fusion | flops 1880096768 | bytes 8650752 | tf_op jit(solution)/shard_map/dot_general | solution.py:14
  440.5 0.0 reduce-scatter.5.cloned.1.call-update
  440.6 0.0 copy-done.3
  440.6 0.0 copy-start.1
  440.6 0.0 copy-start.5
  440.6 7.5 %fusion.7 = bf16[1792,512]{1,0:T(8,128)(2,1)} fusion(bf16[1024,512]{1,0:T(8,128)(2,1)S(1)} %copy-done.3, bf16[1024,1792]{1,0:T(8,128)(2,1)} %get-tuple-element.8, bf16[1024,1792]{1,0:T(8,128)(2,1)} %get-tuple-element.9), kind=kOutput, calls=%fused_computation.11 | convolution fusion | flops 1894645760 | bytes 10223616 | tf_op jit(solution)/shard_map/dot_general | solution.py:8
  448.0 0.0 copy-done.1
  448.0 0.0 copy-done.5
  448.0 3.3 fusion.11
  451.4 0.0 copy-start.6
  451.4 3.9 copy.10
  455.3 0.0 copy-done.6
  455.3 5.4 %fusion.10 = bf16[512,1792]{0,1:T(8,128)(2,1)} fusion(bf16[1024,1792]{1,0:T(8,128)(2,1)} %all-gather.9.cloned.1.call-done, bf16[1024,512]{1,0:T(8,128)(2,1)S(1)} %copy-done.6), kind=kOutput, calls=%fused_computation.14 | convolution fusion | flops 1879965696 | bytes 6553600 | tf_op jit(solution)/shard_map/dot_general | solution.py:8
  460.7 3.8 copy.9
  464.5 30.2 %reduce-scatter.5.cloned.1.call-done = bf16[64,512]{1,0:T(8,128)(2,1)} async-done(((bf16[1024,512]{1,0:T(8,128)(2,1)}), bf16[64,512]{1,0:T(8,128)(2,1)}) %reduce-scatter.5.cloned.1.call-update) | async-done | bytes 65552 | tf_op jit(solution)/shard_map/reduce_scatter | solution.py:63
Async XLA Ops:
  7.2 84.6 %copy-start = (bf16[512,1792]{1,0:T(8,128)(2,1)S(1)}, bf16[512,1792]{1,0:T(8,128)(2,1)}, u32[]{:S(2)}) copy-start(bf16[512,1792]{1,0:T(8,128)(2,1)} %param.7) | copy-start | bytes 5505028
  7.2 45.5 %all-gather.5.cloned.1.call-start = ((), (), s32[]{:S(2)}) async-start(), calls=%async_computation.2 | async-start | bytes 1114112 | tf_op jit(solution)/shard_map/all_gather | solution.py:37
  7.9 83.9 %all-gather.7.cloned.1.call-start = ((), (), s32[]{:S(2)}) async-start(), calls=%async_computation.4 | async-start | bytes 1114112 | tf_op jit(solution)/shard_map/all_gather | solution.py:36
  8.7 165.0 %reduce-scatter.3.cloned.1.call-start = ((), (), s32[]{:S(2)}) async-start(), calls=%async_computation.3 | async-start | bytes 3899392 | tf_op jit(solution)/shard_map/reduce_scatter | solution.py:42
  58.5 261.2 %all-reduce.3.cloned.1.call-start = ((), (), s32[]{:S(2)}) async-start(), calls=%async_computation.8 | async-start | bytes 14680064 | tf_op jit(solution)/shard_map/psum | solution.py:46
  91.8 5.3 %copy-start.2 = (bf16[512,1792]{1,0:T(8,128)(2,1)S(1)}, bf16[512,1792]{1,0:T(8,128)(2,1)}, u32[]{:S(2)}) copy-start(bf16[512,1792]{1,0:T(8,128)(2,1)} %param.8) | copy-start | bytes 5505028
  91.8 5.3 %copy-start.4 = (bf16[1024,512]{1,0:T(8,128)(2,1)S(1)}, bf16[1024,512]{1,0:T(8,128)(2,1)}, u32[]{:S(2)}) copy-start(bf16[1024,512]{1,0:T(8,128)(2,1)} %all-gather.7.cloned.1.call-done) | copy-start | bytes 3145732
  101.0 276.0 %all-gather.9.cloned.1.call-start = ((), (), s32[]{:S(2)}) async-start(), calls=%async_computation.5 | async-start | bytes 3899392 | tf_op jit(solution)/shard_map/all_gather | solution.py:56
  321.9 112.3 %all-gather.11.cloned.1.call-start = ((), (), s32[]{:S(2)}) async-start(), calls=%async_computation.6 | async-start | bytes 3899392 | tf_op jit(solution)/shard_map/all_gather | solution.py:57
  322.5 172.2 %reduce-scatter.5.cloned.1.call-start = ((), (), s32[]{:S(2)}) async-start(), calls=%async_computation.7 | async-start | bytes 1114112 | tf_op jit(solution)/shard_map/reduce_scatter | solution.py:63
  382.5 58.0 %copy-start.3 = (bf16[1024,512]{1,0:T(8,128)(2,1)S(1)}, bf16[1024,512]{1,0:T(8,128)(2,1)}, u32[]{:S(2)}) copy-start(bf16[1024,512]{1,0:T(8,128)(2,1)} %all-gather.5.cloned.1.call-done) | copy-start | bytes 3145732
  440.6 7.5 %copy-start.1 = (bf16[1024,1792]{1,0:T(8,128)(2,1)S(1)}, bf16[1024,1792]{1,0:T(8,128)(2,1)}, u32[]{:S(2)}) copy-start(bf16[1024,1792]{1,0:T(8,128)(2,1)} %all-gather.11.cloned.1.call-done) | copy-start | bytes 11010052
  440.6 7.5 %copy-start.5 = (bf16[1024,512]{1,0:T(8,128)(2,1)S(1)}, bf16[1024,512]{1,0:T(8,128)(2,1)}, u32[]{:S(2)}) copy-start(bf16[1024,512]{1,0:T(8,128)(2,1)} %all-gather.7.cloned.1.call-done) | copy-start | bytes 3145732
  451.4 3.9 copy-start.6
Sparse Core Ops, SparseCore 0:
  9.8 42.7 all-gather.4
  54.5 37.2 all-gather.6
  95.4 78.1 reduce-scatter.2
  177.0 142.7 all-reduce.2
  322.9 54.1 all-gather.8
  380.2 53.9 all-gather.10
  440.7 53.9 reduce-scatter.4
where the time goes:
time: 504 us; the launch traced here: 502 us
  waiting for transfers between devices  434 us (86%)
  matrix products  43 us (9%)
  between operations  14.2 us (3%)
  local copies, waits for them, and re-layouts  7.72 us (2%)
    psum x1, waiting for transfers between devices, body(): lax.psum(up_part.astype(jnp.bfloat16), 'row').astype(jnp.float32)  146 us
    reduce_scatter x1, waiting for transfers between devices, body(): lax.psum_scatter(down_part.astype(jnp.bfloat16), 'row', scatter_dimension...  72.6 us
    all_gather x1, waiting for transfers between devices, body(): lax.all_gather(dgate, 'row', axis=0, tiled=True)  54.3 us
    all_gather x1, waiting for transfers between devices, body(): lax.all_gather(dup, 'row', axis=0, tiled=True)  51.7 us
    all_gather x1, waiting for transfers between devices, body(): lax.all_gather(out_grad, 'col', axis=0, tiled=True)  44 us
    all_gather x1, waiting for transfers between devices, body(): lax.all_gather(tokens, 'col', axis=0, tiled=True)  33.2 us
    reduce_scatter x1, waiting for transfers between devices, body(): lax.psum_scatter(in_part.astype(jnp.bfloat16), 'col', scatter_dimension=0...  30.2 us
    dot_general x3, matrix products, contract_cols(): lax.dot_general(left, right, (((1,), (1,)), ((), ())), preferred_element_...  17.6 us
  transfers between devices with their start and end apart: 7, of which 7 were waited for; matrix products, arithmetic and copies ran while one was open for 9% of the time, Pallas kernels for 0%

commit v1 on v0

v1 whole, which is shorter than its diff:
```python
import functools

import jax
import jax.numpy as jnp
from jax import lax
from jax.experimental import pallas as pl
from jax.experimental.pallas import tpu as pltpu
from jax.sharding import PartitionSpec as P

MESH = pl.DeviceIdType.MESH
BF = jnp.bfloat16
F32 = jnp.float32

RING = 4
CHIPS = 8
CORES = 2
CHUNKS = 4
OWN = 64
SUB = 16
WIDTH = 512
HID = 1792
HALF = HID // 2
CAT = 3 * HALF
TOKENS = 1024

ORDER = (
    ("first", 0), ("fwd", 1), ("part", 1), ("rs_a1", 0), ("fwd", 2), ("part", 2), ("rs_a2", 0),
    ("rs_a1", 1), ("fwd", 3), ("rs_b1", 0), ("part", 3), ("rs_b2", 0), ("rs_a2", 1), ("ag_b1", 0),
    ("rs_a1", 2), ("rs_b1", 1), ("ag_b2", 0), ("rs_b2", 1), ("rs_a2", 2), ("rs_a1", 3), ("ag_b1", 1),
    ("ag_a1", 0), ("rs_b1", 2), ("ag_b2", 1), ("rs_b2", 2), ("rs_a2", 3), ("ag_a2", 0), ("ag_b1", 2),
    ("rs_b1", 3), ("in_part", 0), ("ag_a1", 1), ("ag_b2", 2), ("rs_b2", 3), ("in_send", 0), ("ag_b1", 3),
    ("ag_a2", 1), ("ag_b2", 3), ("in_part", 1), ("ag_a1", 2), ("in_send", 1), ("ag_a2", 2), ("ag_a1", 3),
    ("in_part", 2), ("in_send", 2), ("ag_a2", 3), ("in_part", 3),
)


def dot(left, right, dims):
    return lax.dot_general(left, right, (dims, ((), ())), preferred_element_type=F32)


def kernel(
    tok_in, grd_in, wg_in, wu_in, wd_in, ing_ref, gg_ref, ug_ref, dg_ref,
    tok, grd, tok_t, hid_t, wg, wu, wd, part, gath, relay_a, land_a, relay_b, land_b,
    in_own, in_sib, in_far, out_g, out_u, out_d,
    load_sem, z_send, z_recv, f_send, f_recv, send, recv, i_send, i_recv, j_send, j_recv, out_sem,
):
    row, col = lax.axis_index("row"), lax.axis_index("col")
    x, y = row % RING, row // RING
    z, core = col // CORES, col % CORES
    pa, pb = x + core * (y - x), y + core * (x - y)
    step_a, step_b = 1 + 3 * core, RING - 3 * core

    def at(a, b):
        return (a * step_a + b * step_b, col)

    up_a, down_a, opp_a = (pa + 1) % RING, (pa + 3) % RING, (pa + 2) % RING
    up_b, down_b, opp_b = (pb + 1) % RING, (pb + 3) % RING, (pb + 2) % RING
    dev_up_a, dev_down_a = at(up_a, pb), at(down_a, pb)
    dev_up_b, dev_down_b = at(pa, up_b), at(pa, down_b)
    sibling = (row, z * CORES + 1 - core)

    def far(step):
        return (row, ((z + step) % CHIPS) * CORES + core)

    loads = [
        pltpu.make_async_copy(tok_in, tok.at[0, core], load_sem.at[0]),
        pltpu.make_async_copy(grd_in, grd.at[0, core], load_sem.at[1]),
        pltpu.make_async_copy(wg_in, wg, load_sem.at[2]),
        pltpu.make_async_copy(wu_in, wu, load_sem.at[3]),
        pltpu.make_async_copy(wd_in, wd, load_sem.at[4]),
    ]
    for copy in loads:
        copy.start()

    barrier = pltpu.get_barrier_semaphore()
    peers = [dev_up_a, dev_down_a, dev_up_b, dev_down_b, sibling] + [far(s) for s in range(1, CHIPS)]
    for peer in peers:
        pl.semaphore_signal(barrier, inc=1, device_id=peer, device_id_type=MESH)
    pl.semaphore_wait(barrier, len(peers))

    started = []

    def push(src, dst, send_sem, recv_sem, device):
        copy = pltpu.make_async_remote_copy(
            src_ref=src, dst_ref=dst, send_sem=send_sem, recv_sem=recv_sem,
            device_id=device, device_id_type=MESH,
        )
        copy.start()
        started.append(copy)
        return copy

    from_sib, from_far = {}, {}

    def to_sibling(slot, src_tok, src_grd):
        from_sib[slot] = [
            push(src_tok, tok.at[slot, core], f_send.at[slot, 0], f_recv.at[slot, 0], sibling),
            push(src_grd, grd.at[slot, core], f_send.at[slot, 1], f_recv.at[slot, 1], sibling),
        ]

    def to_far(slot):
        device = far(CHIPS - slot)
        from_far[slot] = [
            push(tok_in, tok.at[slot, core], z_send.at[slot, 0], z_recv.at[slot, 0], device),
            push(grd_in, grd.at[slot, core], z_send.at[slot, 1], z_recv.at[slot, 1], device),
        ]

    to_far(1)
    to_sibling(0, tok_in, grd_in)
    for slot in (2, 7, 3, 6, 4, 5):
        to_far(slot)

    def forward(slot):
        for copy in from_far[slot]:
            copy.wait_recv()
        to_sibling(slot, tok.at[slot, core], grd.at[slot, core])

    def settle(slot):
        for copy in from_sib[slot]:
            copy.wait_recv()

    def partial(j, slot, count):
        rows = count * CORES * OWN
        blocks = rows // (RING * SUB)
        first = (slot - 2 * j) * 2
        tokens = tok[slot:slot + count].reshape(rows, WIDTH)
        grads = grd[slot:slot + count].reshape(rows, WIDTH)
        tok_t[:, slot * 128:slot * 128 + rows] = tokens.T
        for h in range(2):
            cols = slice(h * HALF, (h + 1) * HALF)

            def put(place, value):
                part[j, h, first:first + blocks, :, :, place * HALF:(place + 1) * HALF] = value.astype(
                    BF).reshape(blocks, RING, SUB, HALF)

            put(0, dot(tokens, wg[:, cols], ((1,), (0,))))
            put(1, dot(tokens, wu[:, cols], ((1,), (0,))))
            put(2, dot(grads, wd[cols, :], ((1,), (1,))))

    def scatter_start(j, base, view, relay, land, me_up, me_down, me_opp, to_up, to_down):
        return {
            "r0": push(view(0, me_opp), relay.at[j, 0], send.at[j, base], recv.at[j, base], to_up),
            "r1": push(view(1, me_opp), relay.at[j, 1], send.at[j, base + 1], recv.at[j, base + 1], to_down),
            "u1": push(view(1, me_up), land.at[j, 0, 1], send.at[j, base + 2], recv.at[j, base + 2], to_up),
            "d0": push(view(0, me_down), land.at[j, 1, 0], send.at[j, base + 3], recv.at[j, base + 3], to_down),
        }

    def scatter_relay(j, base, copies, view, add, land, me_up, me_down, to_up, to_down):
        copies["r0"].wait_recv()
        add(0, me_up)
        copies["u0"] = push(view(0, me_up), land.at[j, 0, 0], send.at[j, base + 4], recv.at[j, base + 4], to_up)
        copies["r1"].wait_recv()
        add(1, me_down)
        copies["d1"] = push(view(1, me_down), land.at[j, 1, 1], send.at[j, base + 5], recv.at[j, base + 5], to_down)

    def settle_scatter(copies):
        for name in ("u1", "d0", "u0", "d1"):
            copies[name].wait_recv()

    def gather_start(j, base, view, to_up, to_down):
        return {
            "u0": push(view(0), view(0), send.at[j, base], recv.at[j, base], to_up),
            "d1": push(view(1), view(1), send.at[j, base + 1], recv.at[j, base + 1], to_down),
            "u1": push(view(1), view(1), send.at[j, base + 2], recv.at[j, base + 2], to_up),
            "d0": push(view(0), view(0), send.at[j, base + 3], recv.at[j, base + 3], to_down),
        }

    def gather_relay(j, base, copies, view_down, view_up, to_up, to_down):
        copies["u0"].wait_recv()
        copies["f0"] = push(view_down(0), view_down(0), send.at[j, base + 4], recv.at[j, base + 4], to_up)
        copies["d1"].wait_recv()
        copies["f1"] = push(view_up(1), view_up(1), send.at[j, base + 5], recv.at[j, base + 5], to_down)

    def settle_gather(copies):
        for name in ("u1", "d0", "f0", "f1"):
            copies[name].wait_recv()

    state = {}

    def view_a(j):
        return lambda h, block: part.at[j, h, block]

    def view_b(j):
        return lambda h, block: part.at[j, h, pa, block]

    def begin(j):
        state["ra", j] = scatter_start(
            j, 0, view_a(j), relay_a, land_a, up_a, down_a, opp_a, dev_up_a, dev_down_a)

    def op_first(j):
        for copy in loads:
            copy.wait()
        settle(0)
        partial(0, 0, 1)
        forward(1)
        settle(1)
        partial(0, 1, 1)
        begin(0)

    def op_fwd(j):
        forward(2 * j)
        forward(2 * j + 1)

    def op_part(j):
        settle(2 * j)
        settle(2 * j + 1)
        partial(j, 2 * j, 2)
        begin(j)

    def op_rs_a1(j):
        def add(h, block):
            def some(i, carry):
                total = part[j, h, block, i].astype(F32) + relay_a[j, h, i].astype(F32)
                part[j, h, block, i] = total.astype(BF)
                return carry
            lax.fori_loop(0, RING, some, 0)
        scatter_relay(j, 0, state["ra", j], view_a(j), add, land_a, up_a, down_a, dev_up_a, dev_down_a)

    def op_rs_a2(j):
        settle_scatter(state["ra", j])
        for h in range(2):
            def some(i, carry):
                total = part[j, h, pa, i].astype(F32) + land_a[j, 0, h, i].astype(F32)
                part[j, h, pa, i] = (total + land_a[j, 1, h, i].astype(F32)).astype(BF)
                return carry
            lax.fori_loop(0, RING, some, 0)
        state["rb", j] = scatter_start(
            j, 6, view_b(j), relay_b, land_b, up_b, down_b, opp_b, dev_up_b, dev_down_b)

    def op_rs_b1(j):
        def add(h, block):
            total = part[j, h, pa, block].astype(F32) + relay_b[j, h].astype(F32)
            part[j, h, pa, block] = total.astype(BF)
        scatter_relay(j, 6, state["rb", j], view_b(j), add, land_b, up_b, down_b, dev_up_b, dev_down_b)

    def op_rs_b2(j):
        settle_scatter(state["rb", j])
        for h in range(2):
            def total(place):
                cols = slice(place * HALF, (place + 1) * HALF)
                value = part[j, h, pa, pb, :, cols].astype(F32) + land_b[j, 0, h, :, cols].astype(F32)
                value = value + land_b[j, 1, h, :, cols].astype(F32)
                return value.astype(BF).astype(F32)
            g_val, u_val, d_val = total(0), total(1), total(2)
            sig = 1.0 / (1.0 + jnp.exp(-g_val))
            act = g_val * sig
            gath[h, j, pa, pb, :, 0:HALF] = (act * u_val).astype(BF)
            gath[h, j, pa, pb, :, HALF:2 * HALF] = (d_val * u_val * sig * (1.0 + g_val * (1.0 - sig))).astype(BF)
            gath[h, j, pa, pb, :, 2 * HALF:] = (d_val * act).astype(BF)
        state["gb", j] = gather_start(j, 12, lambda h: gath.at[h, j, pa, pb], dev_up_b, dev_down_b)

    def op_ag_b1(j):
        gather_relay(
            j, 12, state["gb", j], lambda h: gath.at[h, j, pa, down_b], lambda h: gath.at[h, j, pa, up_b],
            dev_up_b, dev_down_b)

    def op_ag_b2(j):
        settle_gather(state["gb", j])
        state["ga", j] = gather_start(j, 18, lambda h: gath.at[h, j, pa], dev_up_a, dev_down_a)

    def op_ag_a1(j):
        gather_relay(
            j, 18, state["ga", j], lambda h: gath.at[h, j, down_a], lambda h: gath.at[h, j, up_a],
            dev_up_a, dev_down_a)

    def op_ag_a2(j):
        settle_gather(state["ga", j])

    def op_in_part(j):
        total = None
        for h in range(2):
            cols = slice(h * HALF, (h + 1) * HALF)
            for place, weight in ((1, wg), (2, wu)):
                value = gath[h, j, :, :, :, place * HALF:(place + 1) * HALF].reshape(256, HALF)
                term = dot(value, weight[:, cols], ((1,), (1,)))
                total = term if total is None else total + term
        in_own[2 * j:2 * j + 2] = total.astype(BF).reshape(2, CORES, OWN, WIDTH)
        state["is", j] = push(
            in_own.at[2 * j:2 * j + 2, 1 - core], in_sib.at[2 * j:2 * j + 2], i_send.at[j], i_recv.at[j], sibling)
        for h in range(2):
            hid_t[h, :, j * 256:(j + 1) * 256] = gath[h, j, :, :, :, 0:HALF].reshape(256, HALF).T

    def op_in_send(j):
        state["is", j].wait_recv()
        for slot in (2 * j, 2 * j + 1):
            value = in_own[slot, core].astype(F32) + in_sib[slot].astype(F32)
            in_own[slot, core] = value.astype(BF)
            if slot:
                state["iz", slot] = push(
                    in_own.at[slot, core], in_far.at[slot], j_send.at[slot], j_recv.at[slot], far(slot))

    ops = dict(
        first=op_first, fwd=op_fwd, part=op_part, rs_a1=op_rs_a1, rs_a2=op_rs_a2, rs_b1=op_rs_b1, rs_b2=op_rs_b2,
        ag_b1=op_ag_b1, ag_b2=op_ag_b2, ag_a1=op_ag_a1, ag_a2=op_ag_a2, in_part=op_in_part, in_send=op_in_send,
    )
    for name, j in ORDER:
        ops[name](j)

    outs = []

    def put_out(src, dst, sem):
        copy = pltpu.make_async_copy(src, dst, sem)
        copy.start()
        outs.append(copy)

    def grads_of(place, out, dst, sem):
        for h in range(2):
            cols = slice(h * HALF, (h + 1) * HALF)
            value = gath[h, :, :, :, :, place * HALF:(place + 1) * HALF].reshape(TOKENS, HALF)
            out[:, cols] = dot(tok_t[...], value, ((1,), (0,))).astype(BF)
        put_out(out, dst, sem)

    grads_of(1, out_g, gg_ref, out_sem.at[0])
    op_in_send(CHUNKS - 1)
    grads_of(2, out_u, ug_ref, out_sem.at[1])
    for h in range(2):
        cols = slice(h * HALF, (h + 1) * HALF)
        out_d[cols, :] = dot(hid_t[h], grd[...].reshape(TOKENS, WIDTH), ((1,), (0,))).astype(BF)
    put_out(out_d, dg_ref, out_sem.at[2])

    total = in_own[0, core].astype(F32)
    for slot in range(1, CHIPS):
        state["iz", slot].wait_recv()
        total = total + in_far[slot].astype(F32)
    ing_ref[...] = total.astype(BF)

    for copy in started:
        copy.wait_send()
    for copy in outs:
        copy.wait()


def body(tokens, out_grad, w_gate, w_up, w_down):
    any_space = pl.BlockSpec(memory_space=pl.ANY)
    dma = pltpu.SemaphoreType.DMA
    vmem = pltpu.VMEM
    return pl.pallas_call(
        kernel,
        out_shape=(
            jax.ShapeDtypeStruct((OWN, WIDTH), BF),
            jax.ShapeDtypeStruct((WIDTH, HID), BF),
            jax.ShapeDtypeStruct((WIDTH, HID), BF),
            jax.ShapeDtypeStruct((HID, WIDTH), BF),
        ),
        in_specs=[any_space] * 5,
        out_specs=(pl.BlockSpec(memory_space=pltpu.VMEM), any_space, any_space, any_space),
        scratch_shapes=[
            vmem((CHIPS, CORES, OWN, WIDTH), BF),
            vmem((CHIPS, CORES, OWN, WIDTH), BF),
            vmem((WIDTH, TOKENS), BF),
            vmem((2, HALF, TOKENS), BF),
            vmem((WIDTH, HID), BF),
            vmem((WIDTH, HID), BF),
            vmem((HID, WIDTH), BF),
            vmem((CHUNKS, 2, RING, RING, SUB, CAT), BF),
            vmem((2, CHUNKS, RING, RING, SUB, CAT), BF),
            vmem((CHUNKS, 2, RING, SUB, CAT), BF),
            vmem((CHUNKS, 2, 2, RING, SUB, CAT), BF),
            vmem((CHUNKS, 2, SUB, CAT), BF),
            vmem((CHUNKS, 2, 2, SUB, CAT), BF),
            vmem((CHIPS, CORES, OWN, WIDTH), BF),
            vmem((CHIPS, OWN, WIDTH), BF),
            vmem((CHIPS, OWN, WIDTH), BF),
            vmem((WIDTH, HID), BF),
            vmem((WIDTH, HID), BF),
            vmem((HID, WIDTH), BF),
            dma((5,)), dma((CHIPS, 2)), dma((CHIPS, 2)), dma((CHIPS, 2)), dma((CHIPS, 2)),
            dma((CHUNKS, 24)), dma((CHUNKS, 24)), dma((CHUNKS,)), dma((CHUNKS,)),
            dma((CHIPS,)), dma((CHIPS,)), dma((3,)),
        ],
        compiler_params=pltpu.CompilerParams(
            collective_id=0, has_side_effects=True, vmem_limit_bytes=60 * 2**20),
        cost_estimate=pl.CostEstimate(
            flops=16 * TOKENS * WIDTH * HID, bytes_accessed=12 * WIDTH * HID, transcendentals=OWN * HID),
    )(tokens, out_grad, w_gate, w_up, w_down)


def solution(mesh):
    placed = (P("col", "row"), P("col", "row"), P("row", "col"), P("row", "col"), P("col", "row"))
    return jax.shard_map(
        body,
        mesh=mesh,
        in_specs=placed,
        out_specs=(P("col", "row"), P("row", "col"), P("row", "col"), P("col", "row")),
        check_vma=False,
    )
```

time: 504 us -> 164 us (0.33)
  waiting for transfers between devices: 434 us -> 0 us
  Pallas kernels: 0 us -> 156 us
  matrix products: 43 us -> 0 us
  between operations: 14.2 us -> 0.64 us
    all_gather x4 -> x0, waiting for transfers between devices: 183 us -> none  [the longest x1 54.3 us: body(): lax.all_gather(dgate, 'row', axis=0, tiled=True)]
    pallas_call x0 -> x1, Pallas kernels: none -> 156 us  [body(): pl.pallas_call(kernel, out_shape=(jax.ShapeDtypeStruct((OWN, WIDTH), BF),...]
    psum x1 -> x0, waiting for transfers between devices: 146 us -> none  [body(): lax.psum(up_part.astype(jnp.bfloat16), 'row').astype(jnp.float32)]
    reduce_scatter x2 -> x0, waiting for transfers between devices: 103 us -> none  [the longest x1 72.6 us: body(): lax.psum_scatter(down_part.astype(jnp.bfloat16), 'row', scatter_dimension...]
    dot_general x8 -> x0, matrix products: 43 us -> none  [the longest x3 17.6 us: contract_cols(): lax.dot_general(left, right, (((1,), (1,)), ((), ())), preferred_element_...]
  transfers between devices with their start and end apart: 7 -> 0, of which waited for: 7 -> 0; matrix products, arithmetic and copies ran while one was open for 9% -> 0% of each run, Pallas kernels for 0% -> 0%
where the time goes in v1:
time: 164 us
  Pallas kernels  156 us (95%)
  local copies, waits for them, and re-layouts  7.85 us (5%)
    pallas_call x1, Pallas kernels, body(): pl.pallas_call(kernel, out_shape=(jax.ShapeDtypeStruct((OWN, WIDTH), BF),...  156 us
    unnamed x8, local copies, waits for them, and re-layouts  7.85 us

profile of v1, /device:TPU:1, one launch (start us, length us, event | category | flops | bytes accessed | tf_op | source)
XLA Modules:
  0.0 164.3 jit_solution(15182012899753929995)
XLA Ops:
  0.6 155.8 %shard_map.84 = (bf16[64,512]{1,0:T(8,128)(2,1)}, bf16[512,1792]{1,0:T(8,128)(2,1)}, bf16[512,1792]{1,0:T(8,128)(2,1)}, bf16[1792,512]{1,0:T(8,128)(2,1)}) custom-call(bf16[64,512]{1,0:T(8,128)(2,1)} %tok_in.1, bf16[64,512]{1,0:T(8,128)(2,1)} %grd_in.1, bf16[512,1792]{1,0:T(8,128)(2,1)} %wg_in.1, bf16[512,1792]{1,0:T(8,128)(2,1)} %wu_in.1, ...), custom_call_target="tpu_custom_call" | custom-call | flops 15032385536 | bytes 11010048 | tf_op jit(solution)/shard_map/pallas_call | solution.py:336
  156.5 1.5 copy.13
  157.9 0.0 copy-start.1
  157.9 3.0 %copy.14 = bf16[512,1792]{1,0:T(8,128)(2,1)} copy(bf16[512,1792]{1,0:T(8,128)(2,1)} %get-tuple-element.9) | data formatting | bytes 3670016
  160.9 0.0 copy-done.1
  160.9 0.0 copy-start
  160.9 1.2 copy.15
  162.2 0.9 copy-done
  163.1 1.2 copy.16
Async XLA Ops:
  157.9 3.0 %copy-start.1 = (bf16[512,1792]{1,0:T(8,128)(2,1)S(1)}, bf16[512,1792]{1,0:T(8,128)(2,1)}, u32[]{:S(2)}) copy-start(bf16[512,1792]{1,0:T(8,128)(2,1)} %get-tuple-element.10) | copy-start | bytes 5505028
  160.9 2.2 %copy-start = (bf16[1792,512]{1,0:T(8,128)(2,1)S(1)}, bf16[1792,512]{1,0:T(8,128)(2,1)}, u32[]{:S(2)}) copy-start(bf16[1792,512]{1,0:T(8,128)(2,1)} %get-tuple-element.11) | copy-start | bytes 5505028

commit v2 on v1

--- a/solution.py
+++ b/solution.py
@@ -23,14 +23,20 @@
 CAT = 3 * HALF
 TOKENS = 1024
 
+CHIP_OF = (0, 1, 2, 5, 3, 4, 6, 7)
+PLACE_OF = tuple(CHIP_OF.index(step) for step in range(CHIPS))
+CHIP_ROWS = CORES * OWN
+RESULTS = ((OWN, WIDTH), (WIDTH, HID), (WIDTH, HID), (HID, WIDTH))
+
 ORDER = (
-    ("first", 0), ("fwd", 1), ("part", 1), ("rs_a1", 0), ("fwd", 2), ("part", 2), ("rs_a2", 0),
-    ("rs_a1", 1), ("fwd", 3), ("rs_b1", 0), ("part", 3), ("rs_b2", 0), ("rs_a2", 1), ("ag_b1", 0),
-    ("rs_a1", 2), ("rs_b1", 1), ("ag_b2", 0), ("rs_b2", 1), ("rs_a2", 2), ("rs_a1", 3), ("ag_b1", 1),
-    ("ag_a1", 0), ("rs_b1", 2), ("ag_b2", 1), ("rs_b2", 2), ("rs_a2", 3), ("ag_a2", 0), ("ag_b1", 2),
-    ("rs_b1", 3), ("in_part", 0), ("ag_a1", 1), ("ag_b2", 2), ("rs_b2", 3), ("in_send", 0), ("ag_b1", 3),
-    ("ag_a2", 1), ("ag_b2", 3), ("in_part", 1), ("ag_a1", 2), ("in_send", 1), ("ag_a2", 2), ("ag_a1", 3),
-    ("in_part", 2), ("in_send", 2), ("ag_a2", 3), ("in_part", 3),
+    ("first", 0), ("zf2", 9), ("far4", 9), ("rs_a1", 0), ("fwd1", 1), ("part", 1), ("zf3", 9), ("far67", 9),
+    ("rs_a2", 0), ("fwd2", 2), ("rs_a1", 1), ("rs_b1", 0), ("part", 2), ("rs_a2", 1), ("rs_a1", 2), ("fwd3", 3),
+    ("part", 3), ("rs_a2", 2), ("rs_a1", 3), ("rs_b2", 0), ("rs_b1", 1), ("rs_b1", 2), ("ag_b1", 0), ("rs_a2", 3),
+    ("rs_b2", 2), ("rs_b2", 1), ("rs_b1", 3), ("ag_b1", 2), ("ag_b2", 0), ("rs_b2", 3), ("ag_b2", 2), ("ag_b1", 3),
+    ("ag_a1", 2), ("ag_b1", 1), ("ag_b2", 3), ("ag_a1", 3), ("ag_b2", 1), ("ag_a2", 3), ("ag_a2", 2), ("in_part", 2),
+    ("in_part", 3), ("ag_a1", 1), ("in_send", 3), ("ag_a1", 0), ("in_send", 2), ("acc_g", 0), ("acc_g", 1),
+    ("acc_u", 0), ("acc_u", 1), ("ag_a2", 1), ("in_part", 1), ("acc_d", 0), ("acc_d", 1), ("in_send", 1),
+    ("ag_a2", 0),
 )
 
 
@@ -39,10 +45,10 @@
 
 
 def kernel(
-    tok_in, grd_in, wg_in, wu_in, wd_in, ing_ref, gg_ref, ug_ref, dg_ref,
+    tok_in, grd_in, wg_in, wu_in, wd_in, ing_ref, out_g, out_u, out_d,
     tok, grd, tok_t, hid_t, wg, wu, wd, part, gath, relay_a, land_a, relay_b, land_b,
-    in_own, in_sib, in_far, out_g, out_u, out_d,
-    load_sem, z_send, z_recv, f_send, f_recv, send, recv, i_send, i_recv, j_send, j_recv, out_sem,
+    in_own, in_sib, in_far,
+    load_sem, z_send, z_recv, f_send, f_recv, send, recv, i_send, i_recv, j_send, j_recv,
 ):
     row, col = lax.axis_index("row"), lax.axis_index("col")
     x, y = row % RING, row // RING
@@ -97,64 +103,85 @@
             push(src_grd, grd.at[slot, core], f_send.at[slot, 1], f_recv.at[slot, 1], sibling),
         ]
 
-    def to_far(slot):
-        device = far(CHIPS - slot)
+    def to_far(step):
+        slot, device = PLACE_OF[step], far(CHIPS - step)
         from_far[slot] = [
             push(tok_in, tok.at[slot, core], z_send.at[slot, 0], z_recv.at[slot, 0], device),
             push(grd_in, grd.at[slot, core], z_send.at[slot, 1], z_recv.at[slot, 1], device),
         ]
 
-    to_far(1)
-    to_sibling(0, tok_in, grd_in)
-    for slot in (2, 7, 3, 6, 4, 5):
-        to_far(slot)
+    def relay_far(step):
+        place, after = PLACE_OF[step], PLACE_OF[step + 1]
+        from_far[after] = [
+            push(tok.at[place, core], tok.at[after, core], z_send.at[after, 0], z_recv.at[after, 0], far(CHIPS - 1)),
+            push(grd.at[place, core], grd.at[after, core], z_send.at[after, 1], z_recv.at[after, 1], far(CHIPS - 1)),
+        ]
 
     def forward(slot):
         for copy in from_far[slot]:
             copy.wait_recv()
         to_sibling(slot, tok.at[slot, core], grd.at[slot, core])
 
+    to_far(1)
+    to_sibling(0, tok_in, grd_in)
+    to_far(5)
+
     def settle(slot):
         for copy in from_sib[slot]:
             copy.wait_recv()
 
-    def partial(j, slot, count):
-        rows = count * CORES * OWN
-        blocks = rows // (RING * SUB)
-        first = (slot - 2 * j) * 2
+    def partial(j, first, count, ready=lambda i: None):
+        slot, rows = 2 * j + first, count * CHIP_ROWS
         tokens = tok[slot:slot + count].reshape(rows, WIDTH)
         grads = grd[slot:slot + count].reshape(rows, WIDTH)
-        tok_t[:, slot * 128:slot * 128 + rows] = tokens.T
         for h in range(2):
             cols = slice(h * HALF, (h + 1) * HALF)
 
             def put(place, value):
-                part[j, h, first:first + blocks, :, :, place * HALF:(place + 1) * HALF] = value.astype(
-                    BF).reshape(blocks, RING, SUB, HALF)
-
+                value = value.astype(BF)
+                for i in range(count):
+                    sub = 2 * (first + i)
+                    part[j, h, :, sub:sub + 2, :, place * HALF:(place + 1) * HALF] = (
+                        value[i * CHIP_ROWS:(i + 1) * CHIP_ROWS].reshape(RING, 2, SUB, HALF))
+
+            if h == 0:
+                ready(0)
             put(0, dot(tokens, wg[:, cols], ((1,), (0,))))
+            if h == 0:
+                ready(1)
             put(1, dot(tokens, wu[:, cols], ((1,), (0,))))
+            if h == 0:
+                ready(2)
             put(2, dot(grads, wd[cols, :], ((1,), (1,))))
+
+    def turn(j):
+        chips = [tok[2 * j + i].reshape(CHIP_ROWS, WIDTH) for i in range(2)]
+        rows = [chips[i][32 * b:32 * b + 32] for b in range(RING) for i in range(2)]
+        tok_t[:, j * 256:(j + 1) * 256] = jnp.concatenate(rows, axis=0).T
 
     def scatter_start(j, base, view, relay, land, me_up, me_down, me_opp, to_up, to_down):
         return {
-            "r0": push(view(0, me_opp), relay.at[j, 0], send.at[j, base], recv.at[j, base], to_up),
-            "r1": push(view(1, me_opp), relay.at[j, 1], send.at[j, base + 1], recv.at[j, base + 1], to_down),
-            "u1": push(view(1, me_up), land.at[j, 0, 1], send.at[j, base + 2], recv.at[j, base + 2], to_up),
-            "d0": push(view(0, me_down), land.at[j, 1, 0], send.at[j, base + 3], recv.at[j, base + 3], to_down),
+            "r0": [push(view(0, me_opp), relay(0), send.at[j, base], recv.at[j, base], to_up)],
+            "r1": [push(view(1, me_opp), relay(1), send.at[j, base + 1], recv.at[j, base + 1], to_down)],
+            "u1": [push(view(1, me_up), land(0, 1), send.at[j, base + 2], recv.at[j, base + 2], to_up)],
+            "d0": [push(view(0, me_down), land(1, 0), send.at[j, base + 3], recv.at[j, base + 3], to_down)],
         }
 
+    def settle_all(copies, *names):
+        for name in names:
+            for copy in copies[name]:
+                copy.wait_recv()
+
     def scatter_relay(j, base, copies, view, add, land, me_up, me_down, to_up, to_down):
-        copies["r0"].wait_recv()
+        settle_all(copies, "r0")
         add(0, me_up)
-        copies["u0"] = push(view(0, me_up), land.at[j, 0, 0], send.at[j, base + 4], recv.at[j, base + 4], to_up)
-        copies["r1"].wait_recv()
+        copies["u0"] = [push(view(0, me_up), land(0, 0), send.at[j, base + 4], recv.at[j, base + 4], to_up)]
+        settle_all(copies, "r1")
         add(1, me_down)
-        copies["d1"] = push(view(1, me_down), land.at[j, 1, 1], send.at[j, base + 5], recv.at[j, base + 5], to_down)
+        copies["d1"] = [push(view(1, me_down), land(1, 1), send.at[j, base + 5], recv.at[j, base + 5], to_down)]
 
     def settle_scatter(copies):
-        for name in ("u1", "d0", "u0", "d1"):
-            copies[name].wait_recv()
+        settle_all(copies, "u1", "d0", "u0", "d1")
 
     def gather_start(j, base, view, to_up, to_down):
         return {
@@ -182,29 +209,68 @@
     def view_b(j):
         return lambda h, block: part.at[j, h, pa, block]
 
+    def land_view(land, j):
+        return lambda side, h: land.at[j, side, h]
+
+    def relay_view(relay, j):
+        return lambda h: relay.at[j, h]
+
     def begin(j):
         state["ra", j] = scatter_start(
-            j, 0, view_a(j), relay_a, land_a, up_a, down_a, opp_a, dev_up_a, dev_down_a)
+            j, 0, view_a(j), relay_view(relay_a, j), land_view(land_a, j), up_a, down_a, opp_a, dev_up_a, dev_down_a)
+
+    def begin_half(j, i):
+        subs = slice(2 * i, 2 * i + 2)
+        copies = scatter_start(
+            j, 24 if i else 0, lambda h, block: part.at[j, h, block, subs], lambda h: relay_a.at[j, h, subs],
+            lambda side, h: land_a.at[j, side, h, subs], up_a, down_a, opp_a, dev_up_a, dev_down_a)
+        if i:
+            copies = {name: state["ra", j][name] + copies[name] for name in copies}
+        state["ra", j] = copies
 
     def op_first(j):
-        for copy in loads:
-            copy.wait()
+        loads[0].wait()
+        loads[1].wait()
         settle(0)
-        partial(0, 0, 1)
+        partial(0, 0, 1, lambda i: loads[2 + i].wait())
+        begin_half(0, 0)
         forward(1)
+        relay_far(1)
         settle(1)
         partial(0, 1, 1)
-        begin(0)
-
-    def op_fwd(j):
-        forward(2 * j)
-        forward(2 * j + 1)
+        begin_half(0, 1)
+        turn(0)
+
+    def op_zf2(j):
+        forward(PLACE_OF[2])
+        relay_far(2)
+
+    def op_far4(j):
+        to_far(4)
+
+    def op_zf3(j):
+        forward(PLACE_OF[3])
+
+    def op_far67(j):
+        to_far(6)
+        to_far(7)
+
+    def op_fwd1(j):
+        forward(PLACE_OF[5])
+
+    def op_fwd2(j):
+        forward(PLACE_OF[4])
+
+    def op_fwd3(j):
+        forward(PLACE_OF[7])
+        forward(PLACE_OF[6])
 
     def op_part(j):
         settle(2 * j)
         settle(2 * j + 1)
-        partial(j, 2 * j, 2)
+        partial(j, 0, 2)
         begin(j)
+        turn(j)
 
     def op_rs_a1(j):
         def add(h, block):
@@ -213,7 +279,8 @@
                 part[j, h, block, i] = total.astype(BF)
                 return carry
             lax.fori_loop(0, RING, some, 0)
-        scatter_relay(j, 0, state["ra", j], view_a(j), add, land_a, up_a, down_a, dev_up_a, dev_down_a)
+        scatter_relay(
+            j, 0, state["ra", j], view_a(j), add, land_view(land_a, j), up_a, down_a, dev_up_a, dev_down_a)
 
     def op_rs_a2(j):
         settle_scatter(state["ra", j])
@@ -224,13 +291,14 @@
                 return carry
             lax.fori_loop(0, RING, some, 0)
         state["rb", j] = scatter_start(
-            j, 6, view_b(j), relay_b, land_b, up_b, down_b, opp_b, dev_up_b, dev_down_b)
+            j, 6, view_b(j), relay_view(relay_b, j), land_view(land_b, j), up_b, down_b, opp_b, dev_up_b, dev_down_b)
 
     def op_rs_b1(j):
         def add(h, block):
             total = part[j, h, pa, block].astype(F32) + relay_b[j, h].astype(F32)
             part[j, h, pa, block] = total.astype(BF)
-        scatter_relay(j, 6, state["rb", j], view_b(j), add, land_b, up_b, down_b, dev_up_b, dev_down_b)
+        scatter_relay(
+            j, 6, state["rb", j], view_b(j), add, land_view(land_b, j), up_b, down_b, dev_up_b, dev_down_b)
 
     def op_rs_b2(j):
         settle_scatter(state["rb", j])
@@ -265,57 +333,101 @@
     def op_ag_a2(j):
         settle_gather(state["ga", j])
 
+    def gathered(h, j, place):
+        cols = slice(place * HALF, (place + 1) * HALF)
+        chips = [gath[h, j, :, 2 * i:2 * i + 2, :, cols].reshape(CHIP_ROWS, HALF) for i in range(2)]
+        return jnp.concatenate(chips, axis=0)
+
+    def in_half(j, i):
+        total = None
+        for h in range(2):
+            cols = slice(h * HALF, (h + 1) * HALF)
+            for place, weight in ((1, wg), (2, wu)):
+                value = gath[h, j, :, 2 * i:2 * i + 2, :, place * HALF:(place + 1) * HALF].reshape(CHIP_ROWS, HALF)
+                term = dot(value, weight[:, cols], ((1,), (1,)))
+                total = term if total is None else total + term
+        slot = 2 * j + i
+        in_own[slot] = total.astype(BF).reshape(CORES, OWN, WIDTH)
+        sem = j if i else CHUNKS
+        return push(in_own.at[slot, 1 - core], in_sib.at[slot], i_send.at[sem], i_recv.at[sem], sibling)
+
+    def pair(slot):
+        value = in_own[slot, core].astype(F32) + in_sib[slot].astype(F32)
+        in_own[slot, core] = value.astype(BF)
+        if slot:
+            state["iz", slot] = push(
+                in_own.at[slot, core], in_far.at[slot], j_send.at[slot], j_recv.at[slot], far(CHIP_OF[slot]))
+
+    def turn_hidden(j):
+        for h in range(2):
+            hid_t[h, :, j * 256:(j + 1) * 256] = gathered(h, j, 0).T
+
     def op_in_part(j):
         total = None
         for h in range(2):
             cols = slice(h * HALF, (h + 1) * HALF)
             for place, weight in ((1, wg), (2, wu)):
-                value = gath[h, j, :, :, :, place * HALF:(place + 1) * HALF].reshape(256, HALF)
-                term = dot(value, weight[:, cols], ((1,), (1,)))
+                term = dot(gathered(h, j, place), weight[:, cols], ((1,), (1,)))
                 total = term if total is None else total + term
         in_own[2 * j:2 * j + 2] = total.astype(BF).reshape(2, CORES, OWN, WIDTH)
         state["is", j] = push(
             in_own.at[2 * j:2 * j + 2, 1 - core], in_sib.at[2 * j:2 * j + 2], i_send.at[j], i_recv.at[j], sibling)
-        for h in range(2):
-            hid_t[h, :, j * 256:(j + 1) * 256] = gath[h, j, :, :, :, 0:HALF].reshape(256, HALF).T
+        turn_hidden(j)
 
     def op_in_send(j):
         state["is", j].wait_recv()
-        for slot in (2 * j, 2 * j + 1):
-            value = in_own[slot, core].astype(F32) + in_sib[slot].astype(F32)
-            in_own[slot, core] = value.astype(BF)
-            if slot:
-                state["iz", slot] = push(
-                    in_own.at[slot, core], in_far.at[slot], j_send.at[slot], j_recv.at[slot], far(slot))
+        for slot in sorted((2 * j, 2 * j + 1), key=lambda p: -min(CHIP_OF[p], CHIPS - CHIP_OF[p])):
+            pair(slot)
+
+    def grads_of(h, place, j, count, out, more=False):
+        cols = slice(h * HALF, (h + 1) * HALF)
+        rows = slice(j * 256, (j + count) * 256)
+        value = gath[h, j:j + count, :, :, :, place * HALF:(place + 1) * HALF].reshape(count * 256, HALF)
+        term = dot(tok_t[:, rows], value, ((1,), (0,)))
+        if more:
+            term = out[:, cols].astype(F32) + term
+        out[:, cols] = term.astype(BF)
+
+    def down_of(h, j, count, more=False):
+        cols = slice(h * HALF, (h + 1) * HALF)
+        rows = slice(j * 256, (j + count) * 256)
+        grads = grd[2 * j:2 * (j + count)].reshape(count * 256, WIDTH)
+        term = dot(hid_t[h, :, rows], grads, ((1,), (0,)))
+        if more:
+            term = out_d[cols, :].astype(F32) + term
+        out_d[cols, :] = term.astype(BF)
+
+    def op_acc_g(h):
+        grads_of(h, 1, 2, 2, out_g)
+
+    def op_acc_u(h):
+        grads_of(h, 2, 2, 2, out_u)
+
+    def op_acc_d(h):
+        down_of(h, 2, 2)
 
     ops = dict(
-        first=op_first, fwd=op_fwd, part=op_part, rs_a1=op_rs_a1, rs_a2=op_rs_a2, rs_b1=op_rs_b1, rs_b2=op_rs_b2,
+        acc_g=op_acc_g, acc_u=op_acc_u, acc_d=op_acc_d,
+        first=op_first, zf2=op_zf2, zf3=op_zf3, far4=op_far4, far67=op_far67, fwd1=op_fwd1, fwd2=op_fwd2, fwd3=op_fwd3,
+        part=op_part, rs_a1=op_rs_a1, rs_a2=op_rs_a2, rs_b1=op_rs_b1, rs_b2=op_rs_b2,
         ag_b1=op_ag_b1, ag_b2=op_ag_b2, ag_a1=op_ag_a1, ag_a2=op_ag_a2, in_part=op_in_part, in_send=op_in_send,
     )
     for name, j in ORDER:
         ops[name](j)
 
-    outs = []
-
-    def put_out(src, dst, sem):
-        copy = pltpu.make_async_copy(src, dst, sem)
-        copy.start()
-        outs.append(copy)
-
-    def grads_of(place, out, dst, sem):
-        for h in range(2):
-            cols = slice(h * HALF, (h + 1) * HALF)
-            value = gath[h, :, :, :, :, place * HALF:(place + 1) * HALF].reshape(TOKENS, HALF)
-            out[:, cols] = dot(tok_t[...], value, ((1,), (0,))).astype(BF)
-        put_out(out, dst, sem)
-
-    grads_of(1, out_g, gg_ref, out_sem.at[0])
-    op_in_send(CHUNKS - 1)
-    grads_of(2, out_u, ug_ref, out_sem.at[1])
+    near = in_half(0, 1)
+    own = in_half(0, 0)
+    near.wait_recv()
+    pair(1)
     for h in range(2):
-        cols = slice(h * HALF, (h + 1) * HALF)
-        out_d[cols, :] = dot(hid_t[h], grd[...].reshape(TOKENS, WIDTH), ((1,), (0,))).astype(BF)
-    put_out(out_d, dg_ref, out_sem.at[2])
+        grads_of(h, 1, 0, 2, out_g, True)
+    turn_hidden(0)
+    own.wait_recv()
+    pair(0)
+    for h in range(2):
+        grads_of(h, 2, 0, 2, out_u, True)
+    for h in range(2):
+        down_of(h, 0, 2, True)
 
     total = in_own[0, core].astype(F32)
     for slot in range(1, CHIPS):
@@ -325,7 +437,14 @@
 
     for copy in started:
         copy.wait_send()
-    for copy in outs:
+
+
+def store(*refs):
+    sems = refs[-1]
+    copies = [pltpu.make_async_copy(refs[i], refs[4 + i], sems.at[i]) for i in range(4)]
+    for copy in copies:
+        copy.start()
+    for copy in copies:
         copy.wait()
 
 
@@ -333,16 +452,12 @@
     any_space = pl.BlockSpec(memory_space=pl.ANY)
     dma = pltpu.SemaphoreType.DMA
     vmem = pltpu.VMEM
-    return pl.pallas_call(
+    placed = [pltpu.with_memory_space_constraint(v, pltpu.HBM) for v in (tokens, out_grad, w_gate, w_up, w_down)]
+    held = pl.pallas_call(
         kernel,
-        out_shape=(
-            jax.ShapeDtypeStruct((OWN, WIDTH), BF),
-            jax.ShapeDtypeStruct((WIDTH, HID), BF),
-            jax.ShapeDtypeStruct((WIDTH, HID), BF),
-            jax.ShapeDtypeStruct((HID, WIDTH), BF),
-        ),
-        in_specs=[any_space] * 5,
-        out_specs=(pl.BlockSpec(memory_space=pltpu.VMEM), any_space, any_space, any_space),
+        out_shape=tuple(vmem(shape, BF) for shape in RESULTS),
+        in_specs=[pl.BlockSpec(memory_space=pltpu.HBM)] * 5,
+        out_specs=(pl.BlockSpec(memory_space=pltpu.VMEM),) * 4,
         scratch_shapes=[
             vmem((CHIPS, CORES, OWN, WIDTH), BF),
             vmem((CHIPS, CORES, OWN, WIDTH), BF),
@@ -360,18 +475,24 @@
             vmem((CHIPS, CORES, OWN, WIDTH), BF),
             vmem((CHIPS, OWN, WIDTH), BF),
             vmem((CHIPS, OWN, WIDTH), BF),
-            vmem((WIDTH, HID), BF),
-            vmem((WIDTH, HID), BF),
-            vmem((HID, WIDTH), BF),
             dma((5,)), dma((CHIPS, 2)), dma((CHIPS, 2)), dma((CHIPS, 2)), dma((CHIPS, 2)),
-            dma((CHUNKS, 24)), dma((CHUNKS, 24)), dma((CHUNKS,)), dma((CHUNKS,)),
-            dma((CHIPS,)), dma((CHIPS,)), dma((3,)),
+            dma((CHUNKS, 28)), dma((CHUNKS, 28)), dma((CHUNKS + 1,)), dma((CHUNKS + 1,)),
+            dma((CHIPS,)), dma((CHIPS,)),
         ],
         compiler_params=pltpu.CompilerParams(
-            collective_id=0, has_side_effects=True, vmem_limit_bytes=60 * 2**20),
+            collective_id=0, has_side_effects=True, vmem_limit_bytes=48 * 2**20),
         cost_estimate=pl.CostEstimate(
             flops=16 * TOKENS * WIDTH * HID, bytes_accessed=12 * WIDTH * HID, transcendentals=OWN * HID),
-    )(tokens, out_grad, w_gate, w_up, w_down)
+    )(*placed)
+    held = [pltpu.with_memory_space_constraint(v, pltpu.VMEM) for v in held]
+    return pl.pallas_call(
+        store,
+        out_shape=tuple(jax.ShapeDtypeStruct(shape, BF) for shape in RESULTS),
+        in_specs=[any_space] * 4,
+        out_specs=(any_space,) * 4,
+        scratch_shapes=[dma((4,))],
+        compiler_params=pltpu.CompilerParams(vmem_limit_bytes=2**20),
+    )(*held)
 
 
 def solution(mesh):

time: 164 us -> 144 us (0.88)
  Pallas kernels: 156 us -> 143 us
  local copies, waits for them, and re-layouts: 7.85 us -> 0 us
    pallas_call x1 -> x2, Pallas kernels: 156 us -> 143 us  [the longest x1 140 us: body(): pl.pallas_call(kernel, out_shape=tuple((vmem(shape, BF) for shape in RESU...]
    unnamed x8 -> x0, local copies, waits for them, and re-layouts: 7.85 us -> none
where the time goes in v2:
time: 144 us
  Pallas kernels  143 us (99%)
    pallas_call x1, Pallas kernels, body(): pl.pallas_call(kernel, out_shape=tuple((vmem(shape, BF) for shape in RESU...  140 us

profile of v2, /device:TPU:1, one launch (start us, length us, event | category | flops | bytes accessed | tf_op | source)
XLA Modules:
  0.0 143.7 jit_solution(9812701403819217945)
XLA Ops:
  0.6 140.4 %shard_map.84 = (bf16[64,512]{1,0:T(8,128)(2,1)S(1)}, bf16[512,1792]{1,0:T(8,128)(2,1)S(1)}, bf16[512,1792]{1,0:T(8,128)(2,1)S(1)}, bf16[1792,512]{1,0:T(8,128)(2,1)S(1)}) custom-call(bf16[64,512]{1,0:T(8,128)(2,1)} %tok_in.1, bf16[64,512]{1,0:T(8,128)(2,1)} %grd_in.1, bf16[512,1792]{1,0:T(8,128)(2,1)} %wg_in.1, bf16[512,1792]{1,0:T(8,128)(2,1)} %wu_in.1, ...), custom_call_target="tpu_custom_call" | custom-call | flops 15032385536 | bytes 11010048 | tf_op jit(solution)/shard_map/pallas_call | solution.py:456
  141.0 2.5 %shard_map.85 = (bf16[64,512]{1,0:T(8,128)(2,1)}, bf16[512,1792]{1,0:T(8,128)(2,1)}, bf16[512,1792]{1,0:T(8,128)(2,1)}, bf16[1792,512]{1,0:T(8,128)(2,1)}) custom-call(bf16[64,512]{1,0:T(8,128)(2,1)S(1)} %get-tuple-element.8.refs_0_, bf16[512,1792]{1,0:T(8,128)(2,1)S(1)} %get-tuple-element.9.refs_1_, bf16[512,1792]{1,0:T(8,128)(2,1)S(1)} %get-tuple-element.10.refs_2_, ...), custom_call_target="tpu_custom_call" | custom-call | tf_op jit(solution)/shard_map/pallas_call | solution.py:488

commit v3 on v2

--- a/solution.py
+++ b/solution.py
@@ -26,17 +26,19 @@
 CHIP_OF = (0, 1, 2, 5, 3, 4, 6, 7)
 PLACE_OF = tuple(CHIP_OF.index(step) for step in range(CHIPS))
 CHIP_ROWS = CORES * OWN
+LAST = 0
+HIDDEN, GRADS = slice(0, HALF), slice(HALF, CAT)
 RESULTS = ((OWN, WIDTH), (WIDTH, HID), (WIDTH, HID), (HID, WIDTH))
 
 ORDER = (
-    ("first", 0), ("zf2", 9), ("far4", 9), ("rs_a1", 0), ("fwd1", 1), ("part", 1), ("zf3", 9), ("far67", 9),
-    ("rs_a2", 0), ("fwd2", 2), ("rs_a1", 1), ("rs_b1", 0), ("part", 2), ("rs_a2", 1), ("rs_a1", 2), ("fwd3", 3),
-    ("part", 3), ("rs_a2", 2), ("rs_a1", 3), ("rs_b2", 0), ("rs_b1", 1), ("rs_b1", 2), ("ag_b1", 0), ("rs_a2", 3),
-    ("rs_b2", 2), ("rs_b2", 1), ("rs_b1", 3), ("ag_b1", 2), ("ag_b2", 0), ("rs_b2", 3), ("ag_b2", 2), ("ag_b1", 3),
-    ("ag_a1", 2), ("ag_b1", 1), ("ag_b2", 3), ("ag_a1", 3), ("ag_b2", 1), ("ag_a2", 3), ("ag_a2", 2), ("in_part", 2),
-    ("in_part", 3), ("ag_a1", 1), ("in_send", 3), ("ag_a1", 0), ("in_send", 2), ("acc_g", 0), ("acc_g", 1),
-    ("acc_u", 0), ("acc_u", 1), ("ag_a2", 1), ("in_part", 1), ("acc_d", 0), ("acc_d", 1), ("in_send", 1),
-    ("ag_a2", 0),
+    ("first", 0), ("zf2", 9), ("rs_a1", 0), ("fwd1", 1), ("far4", 9), ("part", 1), ("zf3", 9), ("rs_a2", 0),
+    ("far67", 9), ("rs_a1", 1), ("rs_b1", 0), ("fwd2", 2), ("part", 2), ("fwd3", 3), ("part", 3), ("rs_a2", 1),
+    ("rs_b2", 0), ("rs_b1", 1), ("rs_a1", 3), ("rs_b2", 1), ("rs_a1", 2), ("ag_b1", 1), ("rs_a2", 3), ("ag_b2", 1),
+    ("rs_b1", 3), ("rs_a2", 2), ("rs_b2", 3), ("ag_a1", 1), ("rs_b1", 2), ("ag_b1", 3), ("rs_b2", 2), ("ag_b2", 3),
+    ("ag_b1", 0), ("ag_b1", 2), ("ag_a1", 3), ("ag_b2", 2), ("ag_a2", 1), ("in_part", 1), ("in_send", 1),
+    ("ag_a1", 2), ("ag_a2", 3), ("ag_b2", 0), ("in_part", 3), ("ag_a2", 2), ("in_send", 3), ("in_part", 2),
+    ("acc_g", 0), ("ag_a1", 0), ("in_send", 2), ("acc_u", 0), ("acc_u", 1), ("acc_g", 1), ("acc_d", 1), ("acc_d", 0),
+    ("drain", 8), ("ag_a2", 0),
 )
 
 
@@ -321,14 +323,31 @@
             j, 12, state["gb", j], lambda h: gath.at[h, j, pa, down_b], lambda h: gath.at[h, j, pa, up_b],
             dev_up_b, dev_down_b)
 
+    def view_last(cols):
+        return lambda h, block=None: gath.at[h, LAST, pa if block is None else block, :, :, cols]
+
     def op_ag_b2(j):
         settle_gather(state["gb", j])
+        if j == LAST:
+            state["ga", j] = gather_start(j, 18, view_last(GRADS), dev_up_a, dev_down_a)
+            return
         state["ga", j] = gather_start(j, 18, lambda h: gath.at[h, j, pa], dev_up_a, dev_down_a)
 
     def op_ag_a1(j):
+        if j == LAST:
+            view = view_last(GRADS)
+            gather_relay(
+                j, 18, state["ga", j], lambda h: view(h, down_a), lambda h: view(h, up_a), dev_up_a, dev_down_a)
+            state["gh", j] = gather_start(j, 28, view_last(HIDDEN), dev_up_a, dev_down_a)
+            return
         gather_relay(
             j, 18, state["ga", j], lambda h: gath.at[h, j, down_a], lambda h: gath.at[h, j, up_a],
             dev_up_a, dev_down_a)
+
+    def op_ag_h(j):
+        view = view_last(HIDDEN)
+        gather_relay(
+            j, 28, state["gh", j], lambda h: view(h, down_a), lambda h: view(h, up_a), dev_up_a, dev_down_a)
 
     def op_ag_a2(j):
         settle_gather(state["ga", j])
@@ -397,6 +416,13 @@
             term = out_d[cols, :].astype(F32) + term
         out_d[cols, :] = term.astype(BF)
 
+    waited = []
+
+    def op_drain(count):
+        for copy in started[len(waited):len(started) - count]:
+            copy.wait_send()
+            waited.append(copy)
+
     def op_acc_g(h):
         grads_of(h, 1, 2, 2, out_g)
 
@@ -407,7 +433,7 @@
         down_of(h, 2, 2)
 
     ops = dict(
-        acc_g=op_acc_g, acc_u=op_acc_u, acc_d=op_acc_d,
+        acc_g=op_acc_g, acc_u=op_acc_u, acc_d=op_acc_d, drain=op_drain,
         first=op_first, zf2=op_zf2, zf3=op_zf3, far4=op_far4, far67=op_far67, fwd1=op_fwd1, fwd2=op_fwd2, fwd3=op_fwd3,
         part=op_part, rs_a1=op_rs_a1, rs_a2=op_rs_a2, rs_b1=op_rs_b1, rs_b2=op_rs_b2,
         ag_b1=op_ag_b1, ag_b2=op_ag_b2, ag_a1=op_ag_a1, ag_a2=op_ag_a2, in_part=op_in_part, in_send=op_in_send,
@@ -415,17 +441,19 @@
     for name, j in ORDER:
         ops[name](j)
 
-    near = in_half(0, 1)
-    own = in_half(0, 0)
+    near = in_half(LAST, 1)
+    op_ag_h(LAST)
+    own = in_half(LAST, 0)
     near.wait_recv()
     pair(1)
     for h in range(2):
         grads_of(h, 1, 0, 2, out_g, True)
-    turn_hidden(0)
+    for h in range(2):
+        grads_of(h, 2, 0, 2, out_u, True)
     own.wait_recv()
     pair(0)
-    for h in range(2):
-        grads_of(h, 2, 0, 2, out_u, True)
+    settle_gather(state["gh", LAST])
+    turn_hidden(LAST)
     for h in range(2):
         down_of(h, 0, 2, True)
 
@@ -435,8 +463,7 @@
         total = total + in_far[slot].astype(F32)
     ing_ref[...] = total.astype(BF)
 
-    for copy in started:
-        copy.wait_send()
+    op_drain(0)
 
 
 def store(*refs):
@@ -476,7 +503,7 @@
             vmem((CHIPS, OWN, WIDTH), BF),
             vmem((CHIPS, OWN, WIDTH), BF),
             dma((5,)), dma((CHIPS, 2)), dma((CHIPS, 2)), dma((CHIPS, 2)), dma((CHIPS, 2)),
-            dma((CHUNKS, 28)), dma((CHUNKS, 28)), dma((CHUNKS + 1,)), dma((CHUNKS + 1,)),
+            dma((CHUNKS, 34)), dma((CHUNKS, 34)), dma((CHUNKS + 1,)), dma((CHUNKS + 1,)),
             dma((CHIPS,)), dma((CHIPS,)),
         ],
         compiler_params=pltpu.CompilerParams(

time: 144 us -> 137 us (0.951)
  Pallas kernels: 143 us -> 136 us
    pallas_call x1, Pallas kernels: 140 us -> 134 us  [body(): pl.pallas_call(kernel, out_shape=tuple((vmem(shape, BF) for shape in RESU...]
where the time goes in v3:
time: 137 us
  Pallas kernels  136 us (99%)
    pallas_call x1, Pallas kernels, body(): pl.pallas_call(kernel, out_shape=tuple((vmem(shape, BF) for shape in RESU...  134 us

profile of v3, /device:TPU:1, one launch (start us, length us, event | category | flops | bytes accessed | tf_op | source)
XLA Modules:
  0.0 137.2 jit_solution(13894017704560847837)
XLA Ops:
  0.6 133.9 %shard_map.84 = (bf16[64,512]{1,0:T(8,128)(2,1)S(1)}, bf16[512,1792]{1,0:T(8,128)(2,1)S(1)}, bf16[512,1792]{1,0:T(8,128)(2,1)S(1)}, bf16[1792,512]{1,0:T(8,128)(2,1)S(1)}) custom-call(bf16[64,512]{1,0:T(8,128)(2,1)} %tok_in.1, bf16[64,512]{1,0:T(8,128)(2,1)} %grd_in.1, bf16[512,1792]{1,0:T(8,128)(2,1)} %wg_in.1, bf16[512,1792]{1,0:T(8,128)(2,1)} %wu_in.1, ...), custom_call_target="tpu_custom_call" | custom-call | flops 15032385536 | bytes 11010048 | tf_op jit(solution)/shard_map/pallas_call | solution.py:483
  134.5 2.5 %shard_map.85 = (bf16[64,512]{1,0:T(8,128)(2,1)}, bf16[512,1792]{1,0:T(8,128)(2,1)}, bf16[512,1792]{1,0:T(8,128)(2,1)}, bf16[1792,512]{1,0:T(8,128)(2,1)}) custom-call(bf16[64,512]{1,0:T(8,128)(2,1)S(1)} %get-tuple-element.8.refs_0_, bf16[512,1792]{1,0:T(8,128)(2,1)S(1)} %get-tuple-element.9.refs_1_, bf16[512,1792]{1,0:T(8,128)(2,1)S(1)} %get-tuple-element.10.refs_2_, ...), custom_call_target="tpu_custom_call" | custom-call | tf_op jit(solution)/shard_map/pallas_call | solution.py:515

commit v4 on v3

--- a/solution.py
+++ b/solution.py
@@ -230,6 +230,21 @@
             copies = {name: state["ra", j][name] + copies[name] for name in copies}
         state["ra", j] = copies
 
+    def relay_half(i):
+        copies = state["ra", 0]
+        ways = (
+            ("r0", 0, up_a, "u0", 0, dev_up_a, 34 if i else 4),
+            ("r1", 1, down_a, "d1", 1, dev_down_a, 35 if i else 5),
+        )
+        for came, h, block, goes, side, device, sem in ways:
+            copies[came][i].wait_recv()
+            for sub in (2 * i, 2 * i + 1):
+                total = part[0, h, block, sub].astype(F32) + relay_a[0, h, sub].astype(F32)
+                part[0, h, block, sub] = total.astype(BF)
+            subs = slice(2 * i, 2 * i + 2)
+            copies.setdefault(goes, []).append(push(
+                part.at[0, h, block, subs], land_a.at[0, side, h, subs], send.at[0, sem], recv.at[0, sem], device))
+
     def op_first(j):
         loads[0].wait()
         loads[1].wait()
@@ -241,6 +256,7 @@
         settle(1)
         partial(0, 1, 1)
         begin_half(0, 1)
+        relay_half(0)
         turn(0)
 
     def op_zf2(j):
@@ -275,6 +291,10 @@
         turn(j)
 
     def op_rs_a1(j):
+        if j == 0:
+            relay_half(1)
+            return
+
         def add(h, block):
             def some(i, carry):
                 total = part[j, h, block, i].astype(F32) + relay_a[j, h, i].astype(F32)
@@ -503,7 +523,7 @@
             vmem((CHIPS, OWN, WIDTH), BF),
             vmem((CHIPS, OWN, WIDTH), BF),
             dma((5,)), dma((CHIPS, 2)), dma((CHIPS, 2)), dma((CHIPS, 2)), dma((CHIPS, 2)),
-            dma((CHUNKS, 34)), dma((CHUNKS, 34)), dma((CHUNKS + 1,)), dma((CHUNKS + 1,)),
+            dma((CHUNKS, 36)), dma((CHUNKS, 36)), dma((CHUNKS + 1,)), dma((CHUNKS + 1,)),
             dma((CHIPS,)), dma((CHIPS,)),
         ],
         compiler_params=pltpu.CompilerParams(

time: 137 us -> 138 us (level)
  no operation moved by 1% of the time
where the time goes in v4:
time: 138 us; the launch traced here: 137 us
  Pallas kernels  137 us (99%)
    pallas_call x1, Pallas kernels, body(): pl.pallas_call(kernel, out_shape=tuple((vmem(shape, BF) for shape in RESU...  134 us

profile of v4, /device:TPU:1, one launch (start us, length us, event | category | flops | bytes accessed | tf_op | source)
XLA Modules:
  0.0 137.5 jit_solution(3534152706347798323)
XLA Ops:
  0.6 134.2 %shard_map.84 = (bf16[64,512]{1,0:T(8,128)(2,1)S(1)}, bf16[512,1792]{1,0:T(8,128)(2,1)S(1)}, bf16[512,1792]{1,0:T(8,128)(2,1)S(1)}, bf16[1792,512]{1,0:T(8,128)(2,1)S(1)}) custom-call(bf16[64,512]{1,0:T(8,128)(2,1)} %tok_in.1, bf16[64,512]{1,0:T(8,128)(2,1)} %grd_in.1, bf16[512,1792]{1,0:T(8,128)(2,1)} %wg_in.1, bf16[512,1792]{1,0:T(8,128)(2,1)} %wu_in.1, ...), custom_call_target="tpu_custom_call" | custom-call | flops 15032385536 | bytes 11010048 | tf_op jit(solution)/shard_map/pallas_call | solution.py:503
  134.8 2.5 %shard_map.85 = (bf16[64,512]{1,0:T(8,128)(2,1)}, bf16[512,1792]{1,0:T(8,128)(2,1)}, bf16[512,1792]{1,0:T(8,128)(2,1)}, bf16[1792,512]{1,0:T(8,128)(2,1)}) custom-call(bf16[64,512]{1,0:T(8,128)(2,1)S(1)} %get-tuple-element.8.refs_0_, bf16[512,1792]{1,0:T(8,128)(2,1)S(1)} %get-tuple-element.9.refs_1_, bf16[512,1792]{1,0:T(8,128)(2,1)S(1)} %get-tuple-element.10.refs_2_, ...), custom_call_target="tpu_custom_call" | custom-call | tf_op jit(solution)/shard_map/pallas_call | solution.py:535
